TPU v7x, 32 devices: a whole 2x2x4 slice. The times are simulated.
32 devices in a mesh: section: 4 (over y, x), dp: 8 (over z, core).
Axes of the slice: x: 2, y: 2, z: 4, core: 2. Of those that a mesh axis runs over, the one named last changes fastest.
Arguments:
- hidden_in: bfloat16 [2, 2048, 1024], P(None, 'dp'), may hold values from -6 to 6
- cotangent: bfloat16 [2, 2048, 1024], P(None, 'dp'), may hold values from -6 to 6
- bucket_len: int32 [2, 8, 4], P(None, 'dp'), may hold values from 1 to 192, 256 in all within a row
- live_mask: int32 [2, 2048], P(None, 'dp'), may hold values 0 or 1
- routes: int32 [2, 2048, 1], P(None, 'dp'), may hold values from 0 to 7; in each aligned block of 256 rows (0 to 255, 256 to 511, ..., all dimensions but the last counted through in order) at most 48 rows name the same one
- ln1_gain: bfloat16 [1024], P(('section', 'dp')), may hold values from 0.5 to 1.5
- ln1_bias: bfloat16 [1024], P(('section', 'dp')), may hold values from -4 to 4
- w_qkv: bfloat16 [1024, 3072], P(('section', 'dp')), may hold values from -0.1875 to 0.1875
- w_attn_out: bfloat16 [1024, 1024], P(('section', 'dp')), may hold values from -0.75 to 0.75
- ln2_gain: bfloat16 [1024], P(('section', 'dp')), may hold values from 0.5 to 1.5
- ln2_bias: bfloat16 [1024], P(('section', 'dp')), may hold values from -4 to 4
- w_up: bfloat16 [1024, 4096], P(('section', 'dp')), may hold values from -0.1875 to 0.1875
- w_down: bfloat16 [4096, 1024], P(('section', 'dp')), may hold values from -0.09375 to 0.09375
- expert_in: bfloat16 [8, 1024, 4096], P('dp', None, 'section'), may hold values from -0.1875 to 0.1875
- expert_out: bfloat16 [8, 4096, 1024], P('dp', 'section'), may hold values from -0.09375 to 0.09375
- expert_gain: bfloat16 [8, 1024], P('dp', 'section'), may hold values from 0.5 to 1.5
- expert_bias: bfloat16 [8, 1024], P('dp', 'section'), may hold values from -4 to 4
- centroids: bfloat16 [8, 1024], P('dp', 'section'), may hold values from -0.09375 to 0.09375
Outputs:
- block_out: bfloat16 [2, 2048, 1024], P(None, 'dp', 'section')
- input_grad: float32 [2, 2048, 1024], P(None, 'dp', 'section')
- grad_ln1_gain: float32 [1024], P(('section', 'dp'))
- grad_ln1_bias: float32 [1024], P(('section', 'dp'))
- grad_w_qkv: float32 [1024, 3072], P(('section', 'dp'))
- grad_w_attn_out: float32 [1024, 1024], P(('section', 'dp'))
- grad_ln2_gain: float32 [1024], P(('section', 'dp'))
- grad_ln2_bias: float32 [1024], P(('section', 'dp'))
- grad_w_up: float32 [1024, 4096], P(('section', 'dp'))
- grad_w_down: float32 [4096, 1024], P(('section', 'dp'))
- grad_expert_in: float32 [8, 1024, 4096], P('dp', None, 'section')
- grad_expert_out: float32 [8, 4096, 1024], P('dp', 'section')
- grad_expert_gain: float32 [8, 1024], P('dp', 'section')
- grad_expert_bias: float32 [8, 1024], P('dp', 'section')
- grad_centroids: float32 [8, 1024], P('dp', 'section')
Inputs may be any that keep to these rules, and one draw needn't show every extreme that they name: `routes`: in each block of 256 slots of a micro-batch (the slots of one index of dp), at most 48 slots name one expert. `bucket_len`: each block's 4 lengths sum to 256.
All inputs are finite; a program needn't handle non-finite values. No bound on the sum of `live_mask` on one device may be relied on, other than what follows from the above.
Results may differ from a plain program's by a relative error of at most 0.013.
Values may be sent and summed in bfloat16 or wider, within the bound.
A program may use at most 448 MiB of HBM per device.

v0:
```python
import functools
import math
import types

import jax
import jax.numpy as jnp
from jax import lax
from jax.experimental import pallas as pl
from jax.experimental.pallas import tpu as pltpu
from jax.sharding import PartitionSpec as P

HEADS = 16
SECTION = "section"
DP = "dp"
epsilon = 1e-05
masked_value = -1e30
f32 = jnp.float32
bf16 = jnp.bfloat16


def norm_parts(values):
    center = values - jnp.mean(values, axis=-1, keepdims=True)
    spread = jnp.mean(center * center, axis=-1, keepdims=True)
    rs = lax.rsqrt(spread + epsilon)
    return center * rs, rs


def gelu_back(pre, grad):
    outputs, pullback = jax.vjp(jax.nn.gelu, pre)
    return pullback(grad)[0]


def dot(a, b):
    return jnp.dot(a, b, preferred_element_type=f32)


def dot_tn(a, b):
    return jnp.einsum("rd,re->de", a, b, preferred_element_type=f32)


def dot_nt(a, b):
    return jnp.einsum("re,de->rd", a, b, preferred_element_type=f32)


def sum_scatter(part):
    return lax.psum_scatter(
        part.astype(bf16), SECTION, scatter_dimension=part.ndim - 1, tiled=True
    ).astype(f32)


def gather_features(part):
    return lax.all_gather(part, SECTION, axis=part.ndim - 1, tiled=True)


def with_collectives(
    hidden_in,
    cotangent,
    bucket_len,
    live_mask,
    routes,
    ln1_gain,
    ln1_bias,
    w_qkv,
    w_attn_out,
    ln2_gain,
    ln2_bias,
    w_up,
    w_down,
    expert_in,
    expert_out,
    expert_gain,
    expert_bias,
    centroids,
):
    sections = lax.axis_size(SECTION)
    groups = lax.axis_size(DP)
    section = lax.axis_index(SECTION)
    micro, rows, width = hidden_in.shape
    quarter = width // sections
    heads = HEADS // sections
    size = width // HEADS
    ff = w_up.shape[1] // sections
    capacity = 3 * rows // (2 * groups)
    shard = w_up.shape[0]
    own_cols = section * quarter

    def mine(values):
        return lax.dynamic_slice_in_dim(values, own_cols, quarter, values.ndim - 1)

    def column_group(weight, pieces):
        cols = weight.shape[1] // (pieces * sections)
        parts = weight.reshape(shard, pieces, sections, cols).transpose(2, 0, 1, 3)
        parts = parts.reshape(sections, shard, pieces * cols)
        parts = lax.all_to_all(parts, SECTION, split_axis=0, concat_axis=0, tiled=True)
        full = lax.all_gather(parts, DP, axis=1, tiled=True)
        return full.reshape(width, pieces * cols)

    def column_group_back(grad, pieces):
        cols = grad.shape[1] // pieces
        parts = grad.astype(bf16).reshape(sections, groups * shard, pieces * cols)
        parts = lax.psum_scatter(parts, DP, scatter_dimension=1, tiled=True)
        parts = lax.all_to_all(parts, SECTION, split_axis=0, concat_axis=0, tiled=True)
        parts = parts.reshape(sections, shard, pieces, cols).transpose(1, 2, 0, 3)
        return parts.reshape(shard, pieces * sections * cols).astype(f32)

    def row_group_back(grad):
        return lax.psum_scatter(
            grad.astype(bf16), DP, scatter_dimension=0, tiled=True
        ).astype(f32)

    vectors = lax.all_gather(
        jnp.stack([ln1_gain, ln1_bias, ln2_gain, ln2_bias]), (SECTION, DP), axis=1, tiled=True
    ).astype(f32)
    gain_one, bias_one, gain_two, bias_two = vectors
    expert_vectors = lax.all_gather(
        jnp.concatenate([expert_gain, expert_bias, centroids]), SECTION, axis=1, tiled=True
    ).astype(f32)
    expert_g, expert_b, centroid = expert_vectors
    wqkv = column_group(w_qkv, 3)
    wo = lax.all_gather(w_attn_out, DP, axis=0, tiled=True)
    wup = column_group(w_up, 1)
    wdown = lax.all_gather(w_down, DP, axis=0, tiled=True)
    win = expert_in[0]
    wout = expert_out[0]

    ends = jnp.cumsum(bucket_len[:, 0, :], axis=-1)
    slot_ids = jnp.arange(rows, dtype=jnp.int32)
    segments = jnp.sum((slot_ids[None, :, None] >= ends[:, None, :]).astype(jnp.int32), axis=-1)
    same = segments[:, :, None] == segments[:, None, :]
    causal = slot_ids[None, None, :] <= slot_ids[None, :, None]
    opened = (live_mask[:, None, :] == 1) | (slot_ids[None, None, :] == slot_ids[None, :, None])
    allowed = (same & causal & opened)[:, None]
    chosen = routes[:, :, 0]
    picks = (chosen[:, :, None] == jnp.arange(groups, dtype=jnp.int32)).astype(jnp.int32)
    ranks = jnp.sum((jnp.cumsum(picks, axis=1) - picks) * picks, axis=2)
    places = chosen * capacity + ranks
    place_ids = jnp.arange(groups * capacity, dtype=jnp.int32)
    picked = (places[:, None, :] == place_ids[None, :, None]).astype(bf16)

    def dispatch(values):
        out = jnp.einsum("mpt,mtf->pmf", picked, values, preferred_element_type=f32).astype(bf16)
        out = out.reshape(groups, capacity * micro, quarter)
        return lax.all_to_all(out, DP, split_axis=0, concat_axis=0, tiled=True)

    def give_back(values):
        out = lax.all_to_all(values, DP, split_axis=0, concat_axis=0, tiled=True)
        out = out.reshape(groups * capacity, micro, quarter)
        return jnp.einsum("mpt,pmf->mtf", picked, out, preferred_element_type=f32)

    dge = gather_features(dispatch(mine(cotangent))).reshape(-1, width).astype(f32)

    x = hidden_in.reshape(micro * rows, width).astype(f32)
    n1, rs1 = norm_parts(x)
    a1 = (n1 * gain_one + bias_one).astype(bf16)
    qkv = dot(a1, wqkv).astype(bf16)
    q, k, v = (
        qkv[:, i * quarter : (i + 1) * quarter].reshape(micro, rows, heads, size) for i in range(3)
    )
    scale = size ** (-0.5)
    raw = jnp.einsum("mqhd,mkhd->mhqk", q, k, preferred_element_type=f32) * scale
    scores = jnp.where(allowed, raw, masked_value)
    weights = jnp.exp(scores - jnp.max(scores, axis=-1, keepdims=True))
    probs = weights / jnp.sum(weights, axis=-1, keepdims=True)
    probs_low = probs.astype(bf16)
    mixed = jnp.einsum("mhqk,mkhd->mqhd", probs_low, v, preferred_element_type=f32)
    o = mixed.reshape(micro * rows, quarter).astype(bf16)
    y1q = (mine(x) + sum_scatter(dot(o, wo))).astype(bf16)
    y1 = gather_features(y1q).astype(f32)
    n2, rs2 = norm_parts(y1)
    a2 = (n2 * gain_two + bias_two).astype(bf16)
    h = dot(a2, wup)
    u = jax.nn.gelu(h).astype(bf16)
    y2q = (y1q.astype(f32) + sum_scatter(dot(u, wdown))).astype(bf16)

    xe = gather_features(dispatch(y2q.reshape(micro, rows, quarter))).reshape(-1, width)
    xe = xe.astype(f32)
    ne, rse = norm_parts(xe)
    en = (ne * expert_g + expert_b).astype(bf16)
    he = dot(en, win)
    ue = jax.nn.gelu(he).astype(bf16)
    fe_part = dot(ue, wout)
    alpha = jax.nn.sigmoid(jnp.sum(xe * centroid, axis=-1, keepdims=True))
    fe = sum_scatter(fe_part)
    ge = (alpha * fe).astype(bf16).reshape(groups, capacity * micro, quarter)
    block_out = (
        y2q.reshape(micro, rows, quarter).astype(f32) + give_back(ge)
    ).astype(bf16)

    dfe = (alpha * dge).astype(bf16)
    due = dot_nt(dfe, wout)
    grad_out = dot_tn(ue, dfe)
    dhe = gelu_back(he, due).astype(bf16)
    grad_in = dot_tn(en, dhe)
    den_part = dot_nt(dhe, win)
    gden = den_part * expert_g
    stats = lax.psum(
        jnp.stack(
            [
                jnp.mean(gden, axis=-1),
                jnp.mean(gden * ne, axis=-1),
                jnp.sum(dge * fe_part, axis=-1),
            ]
        ),
        SECTION,
    )[..., None]
    den = sum_scatter(den_part)
    neq = mine(ne)
    dlogit = stats[2] * alpha * (1.0 - alpha)
    dxe_ln = rse * (mine(expert_g) * den - stats[0] - neq * stats[1])
    dxe = (dxe_ln + dlogit * mine(centroid)).astype(bf16)
    grad_expert_gain = jnp.sum(den * neq, axis=0)
    grad_expert_bias = jnp.sum(den, axis=0)
    grad_centroid = jnp.sum(dlogit * mine(xe), axis=0)
    back = give_back(dxe.reshape(groups, capacity * micro, quarter))
    dy2q = (mine(cotangent).astype(f32) + back).astype(bf16).reshape(micro * rows, quarter)

    dy2 = gather_features(dy2q)
    grad_down = dot_tn(u, dy2)
    dh = gelu_back(h, dot_nt(dy2, wdown)).astype(bf16)
    grad_up = dot_tn(a2, dh)
    da2_part = dot_nt(dh, wup)
    gda2 = da2_part * gain_two
    stats = lax.psum(
        jnp.stack([jnp.mean(gda2, axis=-1), jnp.mean(gda2 * n2, axis=-1)]), SECTION
    )[..., None]
    da2 = sum_scatter(da2_part)
    n2q = mine(n2)
    dy1q = dy2q.astype(f32) + rs2 * (mine(gain_two) * da2 - stats[0] - n2q * stats[1])
    dy1q = dy1q.astype(bf16)
    dy1 = gather_features(dy1q)
    grad_wo = dot_tn(o, dy1)
    do = dot_nt(dy1, wo).astype(bf16).reshape(micro, rows, heads, size)
    dp = jnp.einsum("mqhd,mkhd->mhqk", do, v, preferred_element_type=f32)
    dv = jnp.einsum("mhqk,mqhd->mkhd", probs_low, do, preferred_element_type=f32)
    delta = jnp.sum(probs * dp, axis=-1, keepdims=True)
    ds = (probs * (dp - delta)).astype(bf16)
    dq = jnp.einsum("mhqk,mkhd->mqhd", ds, k, preferred_element_type=f32) * scale
    dk = jnp.einsum("mhqk,mqhd->mkhd", ds, q, preferred_element_type=f32) * scale
    dqkv = jnp.concatenate(
        [part.reshape(micro * rows, quarter) for part in (dq, dk, dv)], axis=1
    ).astype(bf16)
    grad_qkv = dot_tn(a1, dqkv)
    da1_part = dot_nt(dqkv, wqkv)
    gda1 = da1_part * gain_one
    stats = lax.psum(
        jnp.stack([jnp.mean(gda1, axis=-1), jnp.mean(gda1 * n1, axis=-1)]), SECTION
    )[..., None]
    da1 = sum_scatter(da1_part)
    n1q = mine(n1)
    dx = dy1q.astype(f32) + rs1 * (mine(gain_one) * da1 - stats[0] - n1q * stats[1])

    vector_grads = lax.psum_scatter(
        jnp.stack(
            [
                jnp.sum(da1 * n1q, axis=0),
                jnp.sum(da1, axis=0),
                jnp.sum(da2 * n2q, axis=0),
                jnp.sum(da2, axis=0),
            ]
        ),
        DP,
        scatter_dimension=1,
        tiled=True,
    )
    return (
        block_out,
        dx.reshape(micro, rows, quarter),
        vector_grads[0],
        vector_grads[1],
        column_group_back(grad_qkv, 3),
        row_group_back(grad_wo),
        vector_grads[2],
        vector_grads[3],
        column_group_back(grad_up, 1),
        row_group_back(grad_down),
        grad_in[None],
        grad_out[None],
        grad_expert_gain[None],
        grad_expert_bias[None],
        grad_centroid[None],
    )


MESH = pl.DeviceIdType.MESH
KEYS = 101
CHAIN = {
    "y1": 0,
    "y1g": 1,
    "y2": 0,
    "xe": 1,
    "den": 0,
    "dy2": 1,
    "da2": 0,
    "dy1": 1,
    "da1": 0,
}
SHARED = {
    "geb": "y2d",
    "dxb": "cot",
    "fe": "dge",
    "est": "stats",
    "tst": "stats",
    "vs": "v2",
    "gdn": "wdn",
    "gup": "wup",
    "gwo": "wo",
    "gqk": "wqkv",
    "p": "c",
    "n": "near",
    "nf": "near far",
    "f": "far",
}


LEGS = {
    "xe": ("x", "y", "xy", "yx"),
    "den": ("x0", "x2", "y1", "y2", "xy", "yx"),
}


def semaphore_of(k):
    if k[0] in LEGS:
        leg = LEGS[k[0]].index(k[2])
        return ("chain", CHAIN[k[0]], k[1], leg + 1) if leg < 3 else ("leg", k[0], k[1], leg)
    if k[0] in CHAIN:
        return ("chain", CHAIN[k[0]]) + k[1:]
    if k[0] == "q1":
        return ("stats", k[1], k[2]) if k[1] < 2 else ("chain", 1, 0, k[2])
    if k[0] == "v1":
        return "chain", 1, 1, k[1]
    if k[1] == "s":
        return "u1" if k[0] == "gup" else "e1", k[2]
    if k[0] == "tst":
        return ("stats",) + k[2:]
    return tuple(SHARED.get(part, part) for part in k)
CHUNK = 128


def tn(a, b):
    return lax.dot_general(a, b, (((0,), (0,)), ((), ())), preferred_element_type=f32)


def nt(a, b):
    return lax.dot_general(a, b, (((1,), (1,)), ((), ())), preferred_element_type=f32)


def tanh_parts(v):
    root = 0.7978845608028654
    t = jnp.tanh(root * (v + 0.044715 * (v * v * v)))
    return t, root


def gelu_both(v):
    t, root = tanh_parts(v)
    half = 0.5 * (1.0 + t)
    return v * half, half + 0.5 * v * (1.0 - t * t) * root * (1.0 + 0.134145 * (v * v))


def to_rows(columns):
    lane = lax.broadcasted_iota(jnp.int32, (columns[0].shape[0], 128), 1)
    wide = jnp.zeros(lane.shape, f32)
    for i, column in enumerate(columns):
        wide = jnp.where(lane == i, column, wide)
    return wide.T[:8]


def to_columns(rows):
    return jnp.concatenate([rows, jnp.zeros((120, rows.shape[1]), f32)], axis=0).T


def layout(dims):
    S, G, M, T, D, Q, FQ, C, sh, shd = dims
    nz = G // 2
    R = G * C
    heads = HEADS // S
    return dict(
        wqkv=((S, nz, 2, sh, 3 * Q), bf16),
        wo=((nz, 2, sh, D), bf16),
        wup=((S, nz, 2, sh, FQ), bf16),
        wdn=((nz, 2, shd, D), bf16),
        win=((S, nz, 2, sh, FQ), bf16),
        wout=((nz, 2, shd, D), bf16),
        vin=((8, 128), f32),
        ein=((8, Q), f32),
        vg=((S, G, 8, 128), f32),
        vecs=((8, D), f32),
        evec=((8, D), f32),
        mask=((M, T, T), f32),
        perm=((M, R, T), bf16),
        cots=((M, R, Q), bf16),
        y2s=((M, R, Q), bf16),
        ges=((M, R, Q), bf16),
        dxs=((M, R, Q), bf16),
        ger=((M, R, Q), bf16),
        dxr=((M, R, Q), bf16),
        tst=((M, T, 128), f32),
        est=((M, R, 128), f32),
        a1=((M, T, D), bf16),
        a2=((M, T, D), bf16),
        qkv=((M, T, 3 * Q), bf16),
        probs=((M, heads, T, T), f32),
        o=((M, T, Q), bf16),
        y1=((M, T, D), bf16),
        h=((M, T, FQ), f32),
        u=((M, T, FQ), bf16),
        y2q=((M, T, Q), bf16),
        xe=((M, R, D), bf16),
        dge=((M, R, D), bf16),
        en=((M, R, D), bf16),
        ue=((M, R, FQ), bf16),
        dhe=((M, R, FQ), bf16),
        dfe=((M, R, D), bf16),
        slope=((R, FQ), f32),
        fes=((M, S - 1, R, Q), bf16),
        fer=((M, S - 1, R, Q), bf16),
        feo=((M, R, Q), f32),
        dns=((M, S - 1, R, Q), bf16),
        dnr=((M, S - 1, R, Q), bf16),
        dno=((M, R, Q), f32),
        ess=((M, 8, R), f32),
        esr=((M, S - 1, 8, R), f32),
        ts=((M, S - 1, T, Q), bf16),
        r1=((M, S - 1, T, Q), bf16),
        r2=((M, S - 1, T, Q), bf16),
        own=((M, T, Q), f32),
        tss=((2, M, 8, T), f32),
        tsr=((2, M, S - 1, 8, T), f32),
        dy2=((M, T, D), bf16),
        dh=((M, T, FQ), bf16),
        dqkv=((M, T, 3 * Q), bf16),
        gwo=((nz, 2, sh, D), bf16),
        gqk=((S, nz, 2, sh, 3 * Q), bf16),
        bdn=((nz, shd, D), bf16),
        bup=((S, nz, sh, FQ), bf16),
        bwo=((nz, sh, D), bf16),
        bqk=((S, nz, sh, 3 * Q), bf16),
        zdn=((nz - 1, shd, D), bf16),
        zup=((nz - 1, S, sh, FQ), bf16),
        zwo=((nz - 1, sh, D), bf16),
        zqk=((nz - 1, S, sh, 3 * Q), bf16),
        ups=((S, sh, FQ), bf16),
        upr=((S - 1, sh, FQ), bf16),
        qks=((S, sh, 3 * Q), bf16),
        qkr=((S - 1, sh, 3 * Q), bf16),
        stage=((2, 256, D), bf16),
        out=((M, T, Q), bf16),
        dx=((M, T, Q), f32),
        vgo=((8, 128), f32),
        gqk_out=((sh, 3 * D), f32),
        gwo_out=((sh, D), f32),
        gup_out=((sh, S * FQ), f32),
        gdn_out=((shd, D), f32),
        evo=((8, Q), f32),
        vsum=((8, Q), f32),
        vsr=((G - 1, 8, Q), f32),
    )


INPUTS = [
    "hidden",
    "cot",
    "bucket",
    "live",
    "routes",
    "gain_one",
    "bias_one",
    "gain_two",
    "bias_two",
    "gain_e",
    "bias_e",
    "centroid",
    "wqkv_in",
    "wo_in",
    "wup_in",
    "wdn_in",
    "win_in",
    "wout_in",
]
RESULTS = [
    "out",
    "dx",
    "vgo",
    "gqk_out",
    "gwo_out",
    "gup_out",
    "gdn_out",
    "evo",
]
OUTPUTS = ["to_" + name for name in RESULTS] + ["gin_out", "gout_out"]


def block_kernel(dims, names, *args):
    r = types.SimpleNamespace(**dict(zip(names, args)))
    S, G, M, T, D, Q, FQ, C, sh, shd = dims
    nz = G // 2
    R = G * C
    heads = HEADS // S
    size = D // HEADS
    scale = size ** (-0.5)
    s = lax.axis_index(SECTION)
    d = lax.axis_index(DP)
    z = lax.div(d, 2)
    c = lax.rem(d, 2)
    beside = (s, d + 1 - 2 * c)
    near = z + 1 - 2 * lax.rem(z, 2)
    far = lax.rem(z + 2, nz)
    near_far = lax.rem(near + 2, nz)
    beside_x = s + 1 - 2 * lax.rem(s, 2)
    beside_y = lax.rem(s + 2, S)
    across = lax.rem(beside_x + 2, S)

    def sec(i):
        return lax.rem(s + i, S)

    def dpi(j):
        return lax.rem(d + j, G)

    def zi(j):
        return lax.rem(z + j, nz)

    def to_sec(i):
        return (sec(i), d)

    def to_dp(j):
        return (s, dpi(j))

    def to_z(j):
        return (s, zi(j) * 2 + c)

    def col(q, n=Q):
        return pl.ds(pl.multiple_of(q * n, n), n)

    def seats(e):
        return pl.ds(pl.multiple_of(e * C, C), C)

    mine = col(s)
    places = {}
    pending = {}

    def copy(src, dst, k, device):
        i = places.setdefault(semaphore_of(k), len(places))
        return pltpu.make_async_remote_copy(
            src_ref=src,
            dst_ref=dst,
            send_sem=r.ssem.at[i],
            recv_sem=r.rsem.at[i],
            device_id=device,
            device_id_type=MESH,
        )

    def send(src, dst, k, device):
        sent(k)
        pending[semaphore_of(k)] = copy(src, dst, k, device)
        pending[semaphore_of(k)].start()

    def sent(k):
        last = pending.pop(semaphore_of(k), None)
        if last is not None:
            last.wait_send()

    def recv(dst, k):
        copy(dst, dst, k, beside).wait_recv()

    def each(rows, body):
        step = math.gcd(rows, CHUNK)

        @pl.loop(0, rows // step)
        def _(i):
            body(pl.ds(pl.multiple_of(i * step, step), step))

    others = range(1, S)

    def gather_send(ref, m, k):
        for i in others:
            send(ref.at[m, :, mine], ref.at[m, :, mine], (k, m, i), to_sec(i))

    def gather_recv(ref, m, k, then=None):
        for i in others:
            recv(ref.at[m, :, col(sec(S - i))], (k, m, i))
            if then is not None and i == S - 2:
                then()

    def sum_send(tile, out, arrive, own, m, k, before=None, hold=False):
        for i in others:
            if before is not None:
                sent((before, m, i))
            out[m, i - 1] = tile(sec(i)).astype(bf16)
        own[m] = tile(s)
        if not hold:
            sum_start(out, arrive, m, k)

    def sum_start(out, arrive, m, k):
        for i in others:
            send(out.at[m, i - 1], arrive.at[m, i - 1], (k, m, i), to_sec(i))

    def sum_recv(arrive, m, k, then=None):
        for i in others:
            recv(arrive.at[m, i - 1], (k, m, i))
            if then is not None and i == S - 2:
                then()

    def summed(own, arrive, m, rows):
        total = own[m, rows]
        for i in others:
            total += arrive[m, i - 1, rows].astype(f32)
        return total

    top, low = slice(0, R // 2), slice(R // 2, R)

    def legs_send(ref, m, k):
        send(ref.at[m, :, mine], ref.at[m, :, mine], (k, m, "x"), (beside_x, d))
        send(ref.at[m, :, mine], ref.at[m, :, mine], (k, m, "y"), (beside_y, d))

    def legs_pass(ref, m, k):
        recv(ref.at[m, :, col(beside_x)], (k, m, "x"))
        block = ref.at[m, top, col(beside_x)]
        send(block, block, (k, m, "xy"), (beside_y, d))
        recv(ref.at[m, :, col(beside_y)], (k, m, "y"))
        block = ref.at[m, low, col(beside_y)]
        send(block, block, (k, m, "yx"), (beside_x, d))

    def legs_recv(ref, m, k):
        recv(ref.at[m, top, col(across)], (k, m, "xy"))
        recv(ref.at[m, low, col(across)], (k, m, "yx"))

    quarters = (beside_x, beside_y, across)

    def legs_sum_send(tile, out, arrive, own, m, k):
        for i, q in enumerate(quarters):
            out[m, i] = tile(q).astype(bf16)
        own[m] = tile(s)
        for i in (2, 0):
            send(out.at[m, i, top], arrive.at[m, i, top], (k, m, "x" + str(i)), (beside_x, d))
        for i in (2, 1):
            send(out.at[m, i, low], arrive.at[m, i, low], (k, m, "y" + str(i)), (beside_y, d))

    def legs_sum_pass(out, arrive, m, k):
        recv(arrive.at[m, 2, top], (k, m, "x2"))
        both = out[m, 1, top].astype(f32) + arrive[m, 2, top].astype(f32)
        out[m, 1, top] = both.astype(bf16)
        send(out.at[m, 1, top], arrive.at[m, 1, top], (k, m, "xy"), (beside_y, d))
        recv(arrive.at[m, 2, low], (k, m, "y2"))
        both = out[m, 0, low].astype(f32) + arrive[m, 2, low].astype(f32)
        out[m, 0, low] = both.astype(bf16)
        send(out.at[m, 0, low], arrive.at[m, 0, low], (k, m, "yx"), (beside_x, d))

    def legs_sum_recv(arrive, m, k):
        recv(arrive.at[m, 0, top], (k, m, "x0"))
        recv(arrive.at[m, 1, low], (k, m, "y1"))
        recv(arrive.at[m, 1, top], (k, m, "xy"))
        recv(arrive.at[m, 0, low], (k, m, "yx"))

    def dispatch_send(src, dst, m, k):
        dst[m, seats(d), mine] = src[m, seats(d)]
        for j in range(1, G):
            send(src.at[m, seats(dpi(j))], dst.at[m, seats(d), mine], (k, m, j), to_dp(j))

    def dispatch_recv(dst, m, k):
        for j in range(1, G):
            recv(dst.at[m, seats(dpi(G - j)), mine], (k, m, j))

    def return_send(src, dst, m, k):
        dst[m, seats(d)] = src[m, seats(d)]
        for j in range(1, G):
            send(src.at[m, seats(dpi(j))], dst.at[m, seats(d)], (k, m, j), to_dp(j))

    def return_recv(dst, m, k):
        for j in range(1, G):
            recv(dst.at[m, seats(dpi(G - j))], (k, m, j))

    def part(ref, zz, cc):
        return ref.at[:, zz, cc] if len(ref.shape) == 5 else ref.at[zz, cc]

    def weight_start(ref, k):
        send(part(ref, z, c), part(ref, z, c), (k, "far"), (s, far * 2 + c))
        send(part(ref, z, c), part(ref, z, c), (k, "c", 0), beside)

    def weight_next(ref, k):
        send(part(ref, z, c), part(ref, z, c), (k, "near"), (s, near * 2 + c))

    def weight_far(ref, k):
        recv(part(ref, far, c), (k, "far"))
        send(part(ref, far, c), part(ref, far, c), (k, "near far"), (s, near * 2 + c))
        send(part(ref, far, c), part(ref, far, c), (k, "c", 1), beside)

    def weight_near(ref, k):
        recv(part(ref, near, c), (k, "near"))
        send(part(ref, near, c), part(ref, near, c), (k, "c", 2), beside)
        recv(part(ref, near_far, c), (k, "near far"))
        send(part(ref, near_far, c), part(ref, near_far, c), (k, "c", 3), beside)

    def weight_wait(ref, k):
        for i, zz in enumerate((z, far, near, near_far)):
            recv(part(ref, zz, 1 - c), (k, "c", i))

    load_in = pltpu.make_async_copy(r.win_in, r.win, r.lsem.at[0])
    load_out = pltpu.make_async_copy(r.wout_in, r.wout, r.lsem.at[1])

    early = lax.broadcasted_iota(jnp.int32, (T, T), 0)
    late = lax.broadcasted_iota(jnp.int32, (T, T), 1)

    def seat_tokens(m):
        route = r.routes[m]
        expert_ids = lax.broadcasted_iota(jnp.int32, (G, T), 0)
        picks = jnp.where(expert_ids == route, 1.0, 0.0)
        before = jnp.where(early < late, 1.0, 0.0).astype(bf16)
        counts = jnp.dot(picks.astype(bf16), before, preferred_element_type=f32)
        rank = jnp.sum(counts * picks, axis=0, keepdims=True)
        place = route.astype(f32) * float(C) + rank
        seat_ids = lax.broadcasted_iota(jnp.int32, (R, T), 0).astype(f32)
        r.perm[m] = jnp.where(seat_ids == place, 1.0, 0.0).astype(bf16)
        r.cots[m] = jnp.dot(r.perm[m], r.cot[m, :, mine], preferred_element_type=f32).astype(bf16)

    def entry():
        barrier = pltpu.get_barrier_semaphore()
        for i in others:
            pl.semaphore_signal(barrier, inc=1, device_id=to_sec(i), device_id_type=MESH)
        for j in range(1, G):
            pl.semaphore_signal(barrier, inc=1, device_id=to_dp(j), device_id_type=MESH)
        r.vin[...] = jnp.zeros_like(r.vin)
        for i, ref in enumerate((r.gain_one, r.bias_one, r.gain_two, r.bias_two)):
            r.vin[i : i + 1, 0:sh] = ref[...].astype(f32)
        r.ein[...] = jnp.zeros_like(r.ein)
        for i, ref in enumerate((r.gain_e, r.bias_e, r.centroid)):
            r.ein[i : i + 1, :] = ref[...].astype(f32)
        r.vg[s, d] = r.vin[...]
        r.evec[:, mine] = r.ein[...]
        for piece in range(3):
            r.wqkv[s, z, c, :, piece * Q : (piece + 1) * Q] = r.wqkv_in[
                :, pl.ds(pl.multiple_of(piece * D + s * Q, Q), Q)
            ]
        r.wo[z, c] = r.wo_in[...]
        seat_tokens(0)
        seat_tokens(1)
        pl.semaphore_wait(barrier, S + G - 2)
        for i in others:
            send(r.vin, r.vg.at[s, d], ("v1", i), to_sec(i))
        for i in others:
            for piece in range(3):
                src = r.wqkv_in.at[:, pl.ds(pl.multiple_of(piece * D + sec(i) * Q, Q), Q)]
                dst = r.wqkv.at[s, z, c, :, piece * Q : (piece + 1) * Q]
                send(src, dst, ("q1", piece, i), to_sec(i))
        dispatch_send(r.cots, r.dge, 0, "cot")
        dispatch_send(r.cots, r.dge, 1, "cot")
        for i in others:
            recv(r.vg.at[sec(S - i), d], ("v1", i))
        for j in range(1, G):
            send(r.vg.at[:, d], r.vg.at[:, d], ("v2", j), to_dp(j))
        for i in others:
            for piece in range(3):
                recv(r.wqkv.at[sec(S - i), z, c, :, piece * Q : (piece + 1) * Q], ("q1", piece, i))
        weight_start(r.wqkv, "wqkv")
        weight_next(r.wqkv, "wqkv")
        for i in others:
            send(r.wup_in.at[:, col(sec(i), FQ)], r.wup.at[s, z, c], ("u1", i), to_sec(i))
            send(r.ein, r.evec.at[:, mine], ("e1", i), to_sec(i))
        load_in.start()
        load_out.start()

    def mask_tokens(m):
        end = r.bucket[m, 0, 0]
        seg_q = (early >= end).astype(jnp.int32)
        seg_k = (late >= end).astype(jnp.int32)
        for b in range(1, r.bucket.shape[2]):
            end = end + r.bucket[m, 0, b]
            seg_q += (early >= end).astype(jnp.int32)
            seg_k += (late >= end).astype(jnp.int32)
        live = jnp.broadcast_to(r.live[m : m + 1, :], (T, T))
        allowed = (seg_q == seg_k) & (late <= early) & ((live == 1) | (late == early))
        r.mask[m] = jnp.where(allowed, 1.0, 0.0)

    def spread_vectors():
        for j in range(1, G):
            recv(r.vg.at[:, dpi(G - j)], ("v2", j))
        spread_row = lax.broadcasted_iota(jnp.int32, (128, D), 0)
        spread_lane = lax.broadcasted_iota(jnp.int32, (128, D), 1)
        spread = jnp.where(lax.rem(spread_lane, sh) == spread_row, 1.0, 0.0).astype(bf16)
        stacked = r.vg[...].reshape(S * G * 8, 128).astype(bf16)
        wide = jnp.dot(stacked, spread, preferred_element_type=f32)
        row_id = lax.broadcasted_iota(jnp.int32, (S * G * 8, D), 0)
        lane_id = lax.broadcasted_iota(jnp.int32, (S * G * 8, D), 1)
        low = lax.shift_right_logical(row_id, 3) * sh
        wide = jnp.where((lane_id >= low) & (lane_id < low + sh), wide, 0.0)
        r.vecs[...] = jnp.sum(wide.reshape(S * G, 8, D), axis=0)

    def normed(values):
        mean = jnp.mean(values, axis=1, keepdims=True)
        center = values - mean
        rs = lax.rsqrt(jnp.mean(center * center, axis=1, keepdims=True) + epsilon)
        return center * rs, mean, rs

    def norm_tokens(src, dst, m, at):
        gain = r.vecs[2 * at : 2 * at + 1, :]
        bias = r.vecs[2 * at + 1 : 2 * at + 2, :]

        def body(rows):
            n, mean, rs = normed(src[m, rows].astype(f32))
            r.tst[m, rows, 2 * at : 2 * at + 1] = mean
            r.tst[m, rows, 2 * at + 1 : 2 * at + 2] = rs
            dst[m, rows] = (n * gain + bias).astype(bf16)

        each(T, body)

    entry()
    r.wup[s, z, c] = r.wup_in[:, col(s, FQ)]
    r.wdn[z, c] = r.wdn_in[...]
    mask_tokens(0)
    mask_tokens(1)
    for m in range(M):
        dispatch_recv(r.dge, m, "cot")
        gather_send(r.dge, m, "dge")
    weight_far(r.wqkv, "wqkv")
    weight_start(r.wo, "wo")
    weight_next(r.wo, "wo")
    for i in others:
        recv(r.evec.at[:, col(sec(S - i))], ("e1", i))
        recv(r.wup.at[sec(S - i), z, c], ("u1", i))
    weight_start(r.wup, "wup")
    spread_vectors()
    norm_tokens(r.hidden, r.a1, 0, 0)
    norm_tokens(r.hidden, r.a1, 1, 0)
    weight_near(r.wqkv, "wqkv")
    weight_far(r.wo, "wo")
    weight_next(r.wup, "wup")
    weight_wait(r.wqkv, "wqkv")

    def attend(m):
        @pl.loop(0, 3)
        def _(t):
            w = r.wqkv[:, :, :, :, col(t)].reshape(D, Q)
            r.qkv[m, :, col(t)] = jnp.dot(r.a1[m], w, preferred_element_type=f32).astype(bf16)

        for hh in range(heads):
            at = hh * size
            q = r.qkv[m, :, at : at + size]
            k = r.qkv[m, :, Q + at : Q + at + size]
            v = r.qkv[m, :, 2 * Q + at : 2 * Q + at + size]
            scores = jnp.where(r.mask[m] > 0.0, nt(q, k) * scale, masked_value)
            weights = jnp.exp(scores - jnp.max(scores, axis=1, keepdims=True))
            p = weights / jnp.sum(weights, axis=1, keepdims=True)
            r.probs[m, hh] = p
            mixed = jnp.dot(p.astype(bf16), v, preferred_element_type=f32)
            r.o[m, :, at : at + size] = mixed.astype(bf16)

    def y1_tile(m):
        return lambda q: jnp.dot(
            r.o[m], r.wo[:, :, :, col(q)].reshape(Q, Q), preferred_element_type=f32
        )

    def finish_y1(m):
        sum_recv(r.r1, m, "y1")

        def body(rows):
            total = r.hidden[m, rows, mine].astype(f32) + summed(r.own, r.r1, m, rows)
            r.y1[m, rows, mine] = total.astype(bf16)

        each(T, body)
        gather_send(r.y1, m, "y1g")

    attend(0)
    weight_near(r.wo, "wo")
    weight_wait(r.wo, "wo")
    sum_send(y1_tile(0), r.ts, r.r1, r.own, 0, "y1")
    attend(1)
    sum_send(y1_tile(1), r.ts, r.r1, r.own, 1, "y1")
    weight_far(r.wup, "wup")
    weight_start(r.wdn, "wdn")
    weight_next(r.wdn, "wdn")
    finish_y1(0)
    finish_y1(1)
    weight_near(r.wup, "wup")
    weight_wait(r.wup, "wup")

    def up(m):
        gather_recv(r.y1, m, "y1g")
        norm_tokens(r.y1, r.a2, m, 1)

        @pl.loop(0, FQ // Q)
        def _(t):
            w = r.wup[:, :, :, :, col(t)].reshape(D, Q)
            pre = jnp.dot(r.a2[m], w, preferred_element_type=f32)
            value, slope = gelu_both(pre)
            r.u[m, :, col(t)] = value.astype(bf16)
            r.h[m, :, col(t)] = slope

    def y2_tile(m):
        return lambda q: jnp.dot(
            r.u[m], r.wdn[:, :, :, col(q)].reshape(FQ, Q), preferred_element_type=f32
        )

    weight_far(r.wdn, "wdn")
    up(0)
    up(1)
    weight_near(r.wdn, "wdn")
    weight_wait(r.wdn, "wdn")
    sum_send(y2_tile(0), r.ts, r.r2, r.own, 0, "y2", "y1")
    sum_send(y2_tile(1), r.ts, r.r2, r.own, 1, "y2", "y1", hold=True)

    def finish_y2(m):
        sum_recv(r.r2, m, "y2", None if m else lambda: sum_start(r.ts, r.r2, 1, "y2"))

        def body(rows):
            total = r.y1[m, rows, mine].astype(f32) + summed(r.own, r.r2, m, rows)
            r.y2q[m, rows] = total.astype(bf16)

        each(T, body)
        r.y2s[m] = jnp.dot(r.perm[m], r.y2q[m], preferred_element_type=f32).astype(bf16)
        dispatch_send(r.y2s, r.xe, m, "y2d")

    finish_y2(0)
    dispatch_recv(r.xe, 0, "y2d")
    legs_send(r.xe, 0, "xe")
    finish_y2(1)
    legs_pass(r.xe, 0, "xe")
    dispatch_recv(r.xe, 1, "y2d")
    legs_send(r.xe, 1, "xe")
    load_in.wait()
    load_out.wait()

    def expert(m):
        gather_recv(r.dge, m, "dge")
        legs_recv(r.xe, m, "xe")
        gain, bias, centroid = r.evec[0:1, :], r.evec[1:2, :], r.evec[2:3, :]

        def body(rows):
            v = r.xe[m, rows].astype(f32)
            n, mean, rs = normed(v)
            alpha = jax.nn.sigmoid(jnp.sum(v * centroid, axis=1, keepdims=True))
            r.est[m, rows, 0:1] = mean
            r.est[m, rows, 1:2] = rs
            r.est[m, rows, 2:3] = alpha
            r.en[m, rows] = (n * gain + bias).astype(bf16)
            r.dfe[m, rows] = (alpha * r.dge[m, rows].astype(f32)).astype(bf16)

        each(R, body)

        @pl.loop(0, FQ // Q)
        def _(t):
            w = r.win[:, :, :, :, col(t)].reshape(D, Q)
            pre = jnp.dot(r.en[m], w, preferred_element_type=f32)
            value, slope = gelu_both(pre)
            r.ue[m, :, col(t)] = value.astype(bf16)
            r.slope[:, col(t)] = slope

        if m == 0:
            legs_pass(r.xe, 1, "xe")
        else:
            legs_sum_pass(r.dns, r.dnr, 0, "den")
        stats = [jnp.zeros((R, 1), f32) for _ in range(3)]

        def fe_tile(q):
            tile = jnp.dot(
                r.ue[m], r.wout[:, :, :, col(q)].reshape(FQ, Q), preferred_element_type=f32
            )
            stats[2] += jnp.sum(tile * r.dge[m, :, col(q)].astype(f32), axis=1, keepdims=True)
            return tile

        def den_tile(q):
            return nt(r.dhe[m], r.win[q].reshape(Q, FQ))

        @pl.loop(0, FQ // Q)
        def _(t):
            due = nt(r.dfe[m], r.wout[t].reshape(Q, D))
            r.dhe[m, :, col(t)] = (due * r.slope[:, col(t)]).astype(bf16)

        legs_sum_send(den_tile, r.dns, r.dnr, r.dno, m, "den")
        sum_send(fe_tile, r.fes, r.fer, r.feo, m, "fe", hold=True)
        for i, q in enumerate(quarters + (s,)):
            tile = r.dns[m, i].astype(f32) if i < S - 1 else r.dno[m]
            scaled = tile * r.evec[0:1, col(q)]
            n = (r.xe[m, :, col(q)].astype(f32) - r.est[m, :, 0:1]) * r.est[m, :, 1:2]
            stats[0] += jnp.sum(scaled, axis=1, keepdims=True)
            stats[1] += jnp.sum(scaled * n, axis=1, keepdims=True)
        r.ess[m] = to_rows(stats)
        for i in others:
            send(r.ess.at[m], r.esr.at[m, i - 1], ("est", m, i), to_sec(i))

    expert(0)
    expert(1)

    def finish_den(m):
        legs_sum_recv(r.dnr, m, "den")
        total = r.ess[m]
        for i in others:
            recv(r.esr.at[m, i - 1], ("est", m, i))
            total += r.esr[m, i - 1]
        r.est[m, :, 8:16] = to_columns(total)[:, 0:8]
        gain, centroid = r.evec[0:1, mine], r.evec[2:3, mine]
        if m == 0:
            r.evo[...] = jnp.zeros_like(r.evo)

        def body(rows):
            den = r.dno[m, rows] + r.dnr[m, 0, rows].astype(f32) + r.dnr[m, 1, rows].astype(f32)
            xq = r.xe[m, rows, mine].astype(f32)
            rs, alpha = r.est[m, rows, 1:2], r.est[m, rows, 2:3]
            n = (xq - r.est[m, rows, 0:1]) * rs
            m1, m2 = r.est[m, rows, 8:9] * (1.0 / D), r.est[m, rows, 9:10] * (1.0 / D)
            dlogit = r.est[m, rows, 10:11] * alpha * (1.0 - alpha)
            grad = rs * (gain * den - m1 - n * m2) + dlogit * centroid
            r.dxs[m, rows] = grad.astype(bf16)
            r.evo[0:1, :] += jnp.sum(den * n, axis=0, keepdims=True)
            r.evo[1:2, :] += jnp.sum(den, axis=0, keepdims=True)
            r.evo[2:3, :] += jnp.sum(dlogit * xq, axis=0, keepdims=True)

        each(R, body)
        return_send(r.dxs, r.dxr, m, "dxb")

    def finish_fe(m):
        sum_recv(r.fer, m, "fe")

        def body(rows):
            fe = summed(r.feo, r.fer, m, rows)
            r.ges[m, rows] = (r.est[m, rows, 2:3] * fe).astype(bf16)

        each(R, body)
        return_send(r.ges, r.ger, m, "geb")

    def finish_dxe(m):
        return_recv(r.dxr, m, "dxb")
        back = tn(r.perm[m], r.dxr[m])
        r.dy2[m, :, mine] = (r.cot[m, :, mine].astype(f32) + back).astype(bf16)
        gather_send(r.dy2, m, "dy2")

    finish_den(0)
    legs_sum_pass(r.dns, r.dnr, 1, "den")
    finish_dxe(0)
    finish_den(1)

    writes = []
    results = []

    def give(name):
        i = RESULTS.index(name)
        one = pltpu.make_async_copy(getattr(r, name), getattr(r, "to_" + name), r.lsem.at[4 + i])
        one.start()
        results.append(one)

    def expert_weights(left, right, out):
        for t in range(D // 256):
            slot = len(writes) % 2
            if len(writes) >= 2:
                writes[-2].wait()
            rows = slice(t * 256, (t + 1) * 256)
            lhs = left[:, :, rows].reshape(M * R, 256)
            r.stage[slot] = tn(lhs, right[...].reshape(M * R, D)).astype(bf16)
            writes.append(pltpu.make_async_copy(r.stage.at[slot], out.at[rows], r.lsem.at[2 + slot]))
            writes[-1].start()

    give("evo")

    finish_dxe(1)

    def token_stats(m, at, src):
        stats = [jnp.zeros((T, 1), f32) for _ in range(2)]
        mean, rs = r.tst[m, :, 2 * at : 2 * at + 1], r.tst[m, :, 2 * at + 1 : 2 * at + 2]
        for i in range(S):
            q = sec(i)
            tile = r.ts[m, i - 1].astype(f32) if i else r.own[m]
            scaled = tile * r.vecs[2 * at : 2 * at + 1, col(q)]
            n = (src[m, :, col(q)].astype(f32) - mean) * rs
            stats[0] += jnp.sum(scaled, axis=1, keepdims=True)
            stats[1] += jnp.sum(scaled * n, axis=1, keepdims=True)
        return stats

    def stats_send(m, at, stats):
        r.tss[at, m] = to_rows(stats)
        for i in others:
            send(r.tss.at[at, m], r.tsr.at[at, m, i - 1], ("tst", at, m, i), to_sec(i))

    def stats_recv(m, at):
        total = r.tss[at, m]
        for i in others:
            recv(r.tsr.at[at, m, i - 1], ("tst", at, m, i))
            total += r.tsr[at, m, i - 1]
        r.tst[m, :, 8:16] = to_columns(total)[:, 0:8]

    def dense_back(m):
        if m == 0:
            gather_recv(r.dy2, m, "dy2")

        @pl.loop(0, FQ // Q)
        def _(t):
            du = nt(r.dy2[m], r.wdn[t].reshape(Q, D))
            r.dh[m, :, col(t)] = (du * r.h[m, :, col(t)]).astype(bf16)

        sum_send(
            lambda q: nt(r.dh[m], r.wup[q].reshape(Q, FQ)),
            r.ts,
            r.r1,
            r.own,
            m,
            "da2",
            "y2",
            hold=m == 0,
        )
        stats_send(m, 1, token_stats(m, 1, r.y1))

    def norm_back(m, at, src, grad_in, own, arrive, emit):
        gain = r.vecs[2 * at : 2 * at + 1, mine]

        def body(rows):
            grad = summed(own, arrive, m, rows)
            mean, rs = r.tst[m, rows, 2 * at : 2 * at + 1], r.tst[m, rows, 2 * at + 1 : 2 * at + 2]
            n = (src[m, rows, mine].astype(f32) - mean) * rs
            m1, m2 = r.tst[m, rows, 8:9] * (1.0 / D), r.tst[m, rows, 9:10] * (1.0 / D)
            emit(rows, grad_in[m, rows, mine].astype(f32) + rs * (gain * grad - m1 - n * m2))
            r.vsum[2 * at : 2 * at + 1, :] += jnp.sum(grad * n, axis=0, keepdims=True)
            r.vsum[2 * at + 1 : 2 * at + 2, :] += jnp.sum(grad, axis=0, keepdims=True)

        each(T, body)

    def finish_da2(m):
        sum_recv(r.r1, m, "da2")
        stats_recv(m, 1)
        for i in others:
            sent(("y1g", m, i))

        def emit(rows, value):
            r.y1[m, rows, mine] = value.astype(bf16)

        norm_back(m, 1, r.y1, r.dy2, r.own, r.r1, emit)
        gather_send(r.y1, m, "dy1")

    blocks = (near_far, near, far, z)

    def grads_pair(g, b, k):
        for i, zz in enumerate(blocks):
            src = g.at[:, zz, 1 - c] if len(g.shape) == 5 else g.at[zz, 1 - c]
            dst = b.at[:, zz] if len(g.shape) == 5 else b.at[zz]
            send(src, dst, (k, "p", i), beside)

    def grads_add(g, zz, arrive):
        if len(g.shape) == 5:

            @pl.loop(0, S)
            def _(q):
                g[q, zz, c] = (g[q, zz, c].astype(f32) + arrive[q].astype(f32)).astype(bf16)
        else:
            g[zz, c] = (g[zz, c].astype(f32) + arrive[...].astype(f32)).astype(bf16)

    def grads_paired(g, b, k, i):
        zz = blocks[i]
        piece = b.at[:, zz] if len(g.shape) == 5 else b.at[zz]
        recv(piece, (k, "p", i))
        grads_add(g, zz, piece)

    def grads_near(g, b, arrive, k):
        grads_paired(g, b, k, 0)
        send(part(g, near_far, c), arrive.at[1], (k, "nf"), (s, near * 2 + c))
        grads_paired(g, b, k, 1)
        send(part(g, near, c), arrive.at[0], (k, "n"), (s, near * 2 + c))
        for i in range(2, nz):
            grads_paired(g, b, k, i)

    def grads_far(g, arrive, k):
        recv(arrive.at[1], (k, "nf"))
        grads_add(g, far, arrive.at[1])
        send(part(g, far, c), arrive.at[2], (k, "f"), (s, far * 2 + c))

    def grads_near_recv(arrive, k):
        recv(arrive.at[0], (k, "n"))
        recv(arrive.at[2], (k, "f"))
        return 0, 2

    def down_weights():
        for i, t in enumerate(blocks):
            lhs = r.u[:, :, col(t)].reshape(M * T, Q)
            grad = tn(lhs, r.dy2[...].reshape(M * T, D))
            r.wout[t] = grad.astype(bf16).reshape(2, shd, D)
            send(r.wout.at[t, 1 - c], r.bdn.at[t], ("gdn", "p", i), beside)

    def up_weights():
        @pl.loop(0, S)
        def _(t):
            lhs = r.a2[:, :, col(t)].reshape(M * T, Q)
            grad = tn(lhs, r.dh[...].reshape(M * T, FQ))
            r.win[t] = grad.astype(bf16).reshape(nz, 2, sh, FQ)

        grads_pair(r.win, r.bup, "gup")

    def qkv_weights():
        @pl.loop(0, S)
        def _(t):
            lhs = r.a1[:, :, col(t)].reshape(M * T, Q)
            grad = tn(lhs, r.dqkv[...].reshape(M * T, 3 * Q))
            r.gqk[t] = grad.astype(bf16).reshape(nz, 2, sh, 3 * Q)

        grads_pair(r.gqk, r.bqk, "gqk")

    def out_weights():
        grad = tn(r.o[...].reshape(M * T, Q), r.y1[...].reshape(M * T, D))
        r.gwo[...] = grad.astype(bf16).reshape(nz, 2, sh, D)
        grads_pair(r.gwo, r.bwo, "gwo")

    r.vsum[...] = jnp.zeros_like(r.vsum)
    dense_back(0)
    gather_recv(r.dy2, 1, "dy2", lambda: sum_start(r.ts, r.r1, 0, "da2"))
    down_weights()
    grads_near(r.wout, r.bdn, r.zdn, "gdn")
    dense_back(1)
    finish_da2(0)
    up_weights()
    grads_far(r.wout, r.zdn, "gdn")
    finish_da2(1)
    grads_near(r.win, r.bup, r.zup, "gup")

    def attend_back(m):
        if m == 0:
            gather_recv(r.y1, m, "dy1")
        out_grad = nt(r.y1[m], r.wo[...].reshape(Q, D)).astype(bf16)
        for hh in range(heads):
            at = hh * size
            q = r.qkv[m, :, at : at + size]
            k = r.qkv[m, :, Q + at : Q + at + size]
            v = r.qkv[m, :, 2 * Q + at : 2 * Q + at + size]
            go = out_grad[:, at : at + size]
            p = r.probs[m, hh]
            dp = nt(go, v)
            dv = tn(p.astype(bf16), go)
            ds = (p * (dp - jnp.sum(p * dp, axis=1, keepdims=True))).astype(bf16)
            dq = jnp.dot(ds, k, preferred_element_type=f32) * scale
            dk = tn(ds, q) * scale
            r.dqkv[m, :, at : at + size] = dq.astype(bf16)
            r.dqkv[m, :, Q + at : Q + at + size] = dk.astype(bf16)
            r.dqkv[m, :, 2 * Q + at : 2 * Q + at + size] = dv.astype(bf16)
        sum_send(
            lambda q: nt(r.dqkv[m], r.wqkv[q].reshape(Q, 3 * Q)),
            r.ts,
            r.r2,
            r.own,
            m,
            "da1",
            "da2",
            hold=True,
        )
        stats_send(m, 0, token_stats(m, 0, r.hidden))

    def finish_da1(m):
        sum_recv(r.r2, m, "da1")
        stats_recv(m, 0)

        def emit(rows, value):
            r.dx[m, rows] = value

        norm_back(m, 0, r.hidden, r.y1, r.own, r.r2, emit)

    attend_back(0)
    gather_recv(r.y1, 1, "dy1")
    sum_start(r.fes, r.fer, 0, "fe")
    sum_start(r.fes, r.fer, 1, "fe")
    attend_back(1)
    grads_far(r.win, r.zup, "gup")
    qkv_weights()
    grads_near(r.gqk, r.bqk, r.zqk, "gqk")
    out_weights()
    grads_near(r.gwo, r.bwo, r.zwo, "gwo")
    expert_weights(r.en, r.dhe, r.gin_out)
    finish_fe(0)
    sum_start(r.ts, r.r2, 0, "da1")
    sum_start(r.ts, r.r2, 1, "da1")
    grads_far(r.gqk, r.zqk, "gqk")
    grads_far(r.gwo, r.zwo, "gwo")
    finish_fe(1)
    expert_weights(r.ue, r.dfe, r.gout_out)

    def finish_out(m):
        return_recv(r.ger, m, "geb")
        back = tn(r.perm[m], r.ger[m])
        r.out[m] = (r.y2q[m].astype(f32) + back).astype(bf16)


    def row_result(g, arrive, out, k, rows, wait):
        slots = wait(arrive, k)
        mine_part = part(g, z, c)

        def body(at):
            total = mine_part[at].astype(f32)
            for slot in slots:
                total += arrive[slot, at].astype(f32)
            out[at] = total

        each(rows, body)

    def column_send(g, arrive, out, back, k, wait):
        slots = wait(arrive, k)

        @pl.loop(0, S)
        def _(q):
            total = g[q, z, c].astype(f32)
            for slot in slots:
                total += arrive[slot, q].astype(f32)
            out[q] = total.astype(bf16)

        for i in others:
            send(out.at[sec(i)], back.at[i - 1], (k, "s", i), to_sec(i))

    def column_result(sums, back, out, pieces, k):
        width = sums.shape[2] // pieces
        for i in range(S):
            if i:
                recv(back.at[i - 1], (k, "s", i))
            q = sec(S - i) if i else s
            value = (back[i - 1] if i else sums[s]).astype(f32)
            for piece in range(pieces):
                at = pl.ds(pl.multiple_of(piece * S * width + q * width, width), width)
                out[:, at] = value[:, piece * width : (piece + 1) * width]

    row_result(r.wout, r.zdn, r.gdn_out, "gdn", shd, grads_near_recv)
    give("gdn_out")
    column_send(r.win, r.zup, r.ups, r.upr, "gup", grads_near_recv)
    finish_da1(0)
    finish_da1(1)
    give("dx")
    for j in range(1, G):
        send(r.vsum, r.vsr.at[j - 1], ("vs", j), to_dp(j))
    column_send(r.gqk, r.zqk, r.qks, r.qkr, "gqk", grads_near_recv)
    row_result(r.gwo, r.zwo, r.gwo_out, "gwo", sh, grads_near_recv)
    give("gwo_out")
    column_result(r.ups, r.upr, r.gup_out, 1, "gup")
    give("gup_out")
    finish_out(0)
    finish_out(1)
    give("out")
    total = r.vsum[...]
    for j in range(1, G):
        recv(r.vsr.at[j - 1], ("vs", j))
        total += r.vsr[j - 1]
    shard = jnp.zeros((8, sh), f32)
    for j in range(G):
        shard += jnp.where(d == j, 1.0, 0.0) * total[:, j * sh : (j + 1) * sh]
    r.vgo[...] = jnp.zeros_like(r.vgo)
    r.vgo[:, 0:sh] = shard
    give("vgo")
    column_result(r.qks, r.qkr, r.gqk_out, 3, "gqk")
    give("gqk_out")

    def drain():
        for write in writes[-2:] + results:
            write.wait()
        for last in pending.values():
            last.wait_send()

    drain()
    assert len(places) == KEYS, len(places)


def hand_over(*refs):
    (out, dx, vgo, gqk, gwo, gup, gdn, evo, gin, gout) = refs[:10]
    results = refs[10:]
    results[8][...] = gin[...].astype(f32)
    results[9][...] = gout[...].astype(f32)

    @pl.when(pl.program_id(0) == 0)
    def _():
        for src, dst in zip((out, dx, gqk, gwo, gup, gdn), results[:2] + results[4:8]):
            dst[...] = src[...]
        for i, dst in enumerate(results[2:4] + results[10:12]):
            dst[...] = vgo[i : i + 1, 0 : dst.shape[1]]
        for i, dst in enumerate(results[12:]):
            dst[...] = evo[i : i + 1, :]


def with_kernel(
    hidden_in,
    cotangent,
    bucket_len,
    live_mask,
    routes,
    ln1_gain,
    ln1_bias,
    w_qkv,
    w_attn_out,
    ln2_gain,
    ln2_bias,
    w_up,
    w_down,
    expert_in,
    expert_out,
    expert_gain,
    expert_bias,
    centroids,
):
    S = lax.axis_size(SECTION)
    G = lax.axis_size(DP)
    M, T, D = hidden_in.shape
    Q = D // S
    FQ = w_up.shape[1] // S
    C = 3 * T // (2 * G)
    sh, shd = w_up.shape[0], w_down.shape[0]
    dims = (S, G, M, T, D, Q, FQ, C, sh, shd)
    scratch = layout(dims)
    names = INPUTS + OUTPUTS + list(scratch) + ["ssem", "rsem", "lsem"]
    vmem = pl.BlockSpec(memory_space=pltpu.VMEM)
    smem = pl.BlockSpec(memory_space=pltpu.SMEM)
    anywhere = pl.BlockSpec(memory_space=pl.ANY)
    shapes = (
        ((M, T, Q), bf16),
        ((M, T, Q), f32),
        ((8, 128), f32),
        ((sh, 3 * D), f32),
        ((sh, D), f32),
        ((sh, S * FQ), f32),
        ((shd, D), f32),
        ((8, Q), f32),
        ((D, FQ), bf16),
        ((FQ, D), bf16),
    )
    outs = pl.pallas_call(
        functools.partial(block_kernel, dims, names),
        name="block",
        out_shape=[jax.ShapeDtypeStruct(*shape) for shape in shapes],
        in_specs=[vmem, vmem, smem] + [vmem] * 13 + [anywhere] * 2,
        out_specs=[anywhere] * len(shapes),
        scratch_shapes=[pltpu.VMEM(*shape) for shape in scratch.values()]
        + [pltpu.SemaphoreType.DMA((KEYS,))] * 2
        + [pltpu.SemaphoreType.DMA((4 + len(RESULTS),))],
        compiler_params=pltpu.CompilerParams(
            collective_id=0, has_side_effects=True, vmem_limit_bytes=63 << 20
        ),
    )(
        hidden_in,
        cotangent,
        bucket_len,
        live_mask,
        jnp.swapaxes(routes, 1, 2),
        ln1_gain.reshape(1, sh),
        ln1_bias.reshape(1, sh),
        ln2_gain.reshape(1, sh),
        ln2_bias.reshape(1, sh),
        expert_gain,
        expert_bias,
        centroids,
        w_qkv,
        w_attn_out,
        w_up,
        w_down,
        expert_in.reshape(S, G // 2, 2, sh, FQ),
        expert_out.reshape(G // 2, 2, shd, D),
    )

    def spec(shape):
        if shape in ((D, FQ), (FQ, D)):
            return pl.BlockSpec((256, shape[1]), lambda i: (i, 0))
        return pl.BlockSpec(shape, lambda i, n=len(shape): (0,) * n)

    finals = (
        shapes[:2]
        + (((1, sh), f32),) * 2
        + shapes[3:7]
        + (((D, FQ), f32), ((FQ, D), f32))
        + (((1, sh), f32),) * 2
        + (((1, Q), f32),) * 3
    )
    outs = pl.pallas_call(
        hand_over,
        name="hand_over",
        grid=(D // 256,),
        out_shape=[jax.ShapeDtypeStruct(*shape) for shape in finals],
        in_specs=[spec(shape) for shape, _ in shapes],
        out_specs=[spec(shape) for shape, _ in finals],
        compiler_params=pltpu.CompilerParams(vmem_limit_bytes=63 << 20),
    )(*outs)
    out, dx, gain1, bias1, gqkv, gwo, gup, gdn, gin, gout, gain2, bias2, eg, eb, ec = outs
    return (
        out,
        dx,
        gain1.reshape(sh),
        bias1.reshape(sh),
        gqkv,
        gwo,
        gain2.reshape(sh),
        bias2.reshape(sh),
        gup,
        gdn,
        gin[None],
        gout[None],
        eg,
        eb,
        ec,
    )


def on_device(*args):
    groups = lax.axis_size(DP)
    rows, shard = args[0].shape[1], args[11].shape[0]
    capacity = 3 * rows // (2 * groups)
    if capacity % 16 or shard % 16 or groups != 8:
        return with_collectives(*args)
    return with_kernel(*args)


def solution(mesh):
    everywhere = (SECTION, DP)
    tokens = P(None, DP, None)
    outs = P(None, DP, SECTION)
    per_expert = P(DP, SECTION)
    return jax.shard_map(
        on_device,
        mesh=mesh,
        in_specs=(
            tokens,
            tokens,
            tokens,
            P(None, DP),
            tokens,
            P(everywhere),
            P(everywhere),
            P(everywhere, None),
            P(everywhere, None),
            P(everywhere),
            P(everywhere),
            P(everywhere, None),
            P(everywhere, None),
            P(DP, None, SECTION),
            P(DP, SECTION, None),
            per_expert,
            per_expert,
            per_expert,
        ),
        out_specs=(
            outs,
            outs,
            P(everywhere),
            P(everywhere),
            P(everywhere, None),
            P(everywhere, None),
            P(everywhere),
            P(everywhere),
            P(everywhere, None),
            P(everywhere, None),
            P(DP, None, SECTION),
            P(DP, SECTION, None),
            per_expert,
            per_expert,
            per_expert,
        ),
        check_vma=False,
    )
```

profile of v0, /device:TPU:0, one launch (start us, length us, event | category | flops | bytes accessed | tf_op | source)
XLA Modules:
  0.0 214.6 jit_solution(6261365543020227190)
XLA Ops:
  0.7 206.2 %block.1 = (bf16[2,256,256]{2,1,0:T(8,128)(2,1)}, f32[2,256,256]{2,1,0:T(8,128)}, f32[8,128]{1,0:T(8,128)}, f32[32,3072]{1,0:T(8,128)}, f32[32,1024]{1,0:T(8,128...) custom-call(bf16[2,256,1024]{2,1,0:T(8,128)(2,1)} %args_0_.4, ...), custom_call_target="tpu_custom_call" | custom-call | tf_op jit(solution)/shard_map/block/pallas_call | solution.py:1408
  206.9 7.6 %hand_over.1 = (bf16[2,256,256]{2,1,0:T(8,128)(2,1)}, f32[2,256,256]{2,1,0:T(8,128)}, f32[1,32]{1,0:T(1,128)}, f32[1,32]{1,0:T(1,128)}, f32[32,3072]{1,0:T(8,128...) custom-call(bf16[2,256,256]{2,1,0:T(8,128)(2,1)} %get-tuple-element., ...), custom_call_target="tpu_custom_call" | custom-call | tf_op jit(solution)/shard_map/hand_over/pallas_call | solution.py:1454
where the time goes:
time: 215 us
  Pallas kernels  214 us (100%)
    pallas_call x1, Pallas kernels, with_kernel(): pl.pallas_call(functools.partial(block_kernel, dims, names), name='block'...  206 us
    pallas_call x1, Pallas kernels, with_kernel(): pl.pallas_call(hand_over, name='hand_over', grid=(D // 256,), out_shape=[...  7.61 us

commit v1 on v0

--- a/solution.py
+++ b/solution.py
@@ -741,7 +741,6 @@
                 dst = r.wqkv.at[s, z, c, :, piece * Q : (piece + 1) * Q]
                 send(src, dst, ("q1", piece, i), to_sec(i))
         dispatch_send(r.cots, r.dge, 0, "cot")
-        dispatch_send(r.cots, r.dge, 1, "cot")
         for i in others:
             recv(r.vg.at[sec(S - i), d], ("v1", i))
         for j in range(1, G):
@@ -751,6 +750,7 @@
                 recv(r.wqkv.at[sec(S - i), z, c, :, piece * Q : (piece + 1) * Q], ("q1", piece, i))
         weight_start(r.wqkv, "wqkv")
         weight_next(r.wqkv, "wqkv")
+        dispatch_send(r.cots, r.dge, 1, "cot")
         for i in others:
             send(r.wup_in.at[:, col(sec(i), FQ)], r.wup.at[s, z, c], ("u1", i), to_sec(i))
             send(r.ein, r.evec.at[:, mine], ("e1", i), to_sec(i))
@@ -1440,7 +1440,7 @@
 
     def spec(shape):
         if shape in ((D, FQ), (FQ, D)):
-            return pl.BlockSpec((256, shape[1]), lambda i: (i, 0))
+            return pl.BlockSpec((512, shape[1]), lambda i: (i, 0))
         return pl.BlockSpec(shape, lambda i, n=len(shape): (0,) * n)
 
     finals = (
@@ -1454,7 +1454,7 @@
     outs = pl.pallas_call(
         hand_over,
         name="hand_over",
-        grid=(D // 256,),
+        grid=(D // 512,),
         out_shape=[jax.ShapeDtypeStruct(*shape) for shape in finals],
         in_specs=[spec(shape) for shape, _ in shapes],
         out_specs=[spec(shape) for shape, _ in finals],

time: 215 us -> 213 us (level)
  no operation moved by 1% of the time
where the time goes in v1:
time: 213 us
  Pallas kernels  212 us (100%)
    pallas_call x1, Pallas kernels, with_kernel(): pl.pallas_call(functools.partial(block_kernel, dims, names), name='block'...  205 us
    pallas_call x1, Pallas kernels, with_kernel(): pl.pallas_call(hand_over, name='hand_over', grid=(D // 512,), out_shape=[...  6.78 us

profile of v1, /device:TPU:0, one launch (start us, length us, event | category | flops | bytes accessed | tf_op | source)
XLA Modules:
  0.0 213.1 jit_solution(1960979796077245030)
XLA Ops:
  0.7 205.4 %block.1 = (bf16[2,256,256]{2,1,0:T(8,128)(2,1)}, f32[2,256,256]{2,1,0:T(8,128)}, f32[8,128]{1,0:T(8,128)}, f32[32,3072]{1,0:T(8,128)}, f32[32,1024]{1,0:T(8,128...) custom-call(bf16[2,256,1024]{2,1,0:T(8,128)(2,1)} %args_0_.4, ...), custom_call_target="tpu_custom_call" | custom-call | tf_op jit(solution)/shard_map/block/pallas_call | solution.py:1408
  206.1 6.8 %hand_over.1 = (bf16[2,256,256]{2,1,0:T(8,128)(2,1)}, f32[2,256,256]{2,1,0:T(8,128)}, f32[1,32]{1,0:T(1,128)}, f32[1,32]{1,0:T(1,128)}, f32[32,3072]{1,0:T(8,128...) custom-call(bf16[2,256,256]{2,1,0:T(8,128)(2,1)} %get-tuple-element., ...), custom_call_target="tpu_custom_call" | custom-call | tf_op jit(solution)/shard_map/hand_over/pallas_call | solution.py:1454
